TPU v7x, 32 devices: a whole 2x2x4 slice. The times are simulated.
32 devices in a mesh: group: 2 (over x), slab: 16 (over z, y, core).
Axes of the slice: x: 2, y: 2, z: 4, core: 2. Of those that a mesh axis runs over, the one named last changes fastest.
Arguments:
- green: bfloat16 [2, 16, 2, 256, 256], P('group', 'slab'), parts along dimension 0
- couplings: bfloat16 [16, 2, 256, 256], P('slab')
- gamma: float32 [16, 256], P('slab'), may hold values from 0.01 to 0.1
- occupation: float32 [2, 16], P('group', 'slab'), parts along dimension 0, may hold values from 0 to 1
- lead_occ: float32 [2], P('group'), parts along dimension 0, may hold values from 0.5 to 1.5
- energy_weight: float32 [2], P('group'), parts along dimension 0, may hold values from 0.5 to 2
Outputs:
- left_lesser: float32 [2, 16, 2, 256, 256], P('group', 'slab'), parts along dimension 0
- currents: float32 [32], P(('group', 'slab')), parts along dimension 0
There are 2 independent parts, one for each index of `group`. A program takes and returns all parts, laid end to end along the dimension named above; an argument that names none is the same for every part. Nothing has to cross between parts.
All inputs are finite; a program needn't handle non-finite values.
Results may differ from a plain program's by a relative error of at most 0.0003.
Values sent between devices are 32-bit elements; how exact they have to be, the bound alone decides.
A program may use at most 256 MiB of HBM per device.

v0:
```python
import jax
import jax.numpy as jnp
from jax import lax
from jax.sharding import PartitionSpec as P


def carried_in(array, axis, combine, identity, reverse):
    count, index = (lax.axis_size(axis), lax.axis_index(axis))
    everything = jax.tree.map(lambda part: lax.all_gather(part, axis), array)
    start = jax.tree.map(
        lambda part, zero: jnp.broadcast_to(jnp.asarray(zero, part.dtype), part.shape),
        array,
        identity,
    )

    def hop(k, before):
        at = count - 1 - k if reverse else k
        reached = at > index if reverse else at < index
        new = combine(before, jax.tree.map(lambda part: part[at], everything))
        return jax.tree.map(lambda a, b: jnp.where(reached, a, b), new, before)

    return lax.fori_loop(0, count, hop, start)


def mult(left, right):
    return jnp.einsum(
        "eij,ejk->eik",
        left,
        right,
        preferred_element_type=jnp.float32,
        precision=lax.Precision.HIGHEST,
    )


def cdot(left, right):
    real_part = mult(left[:, 0], right[:, 0]) - mult(left[:, 1], right[:, 1])
    imag_part = mult(left[:, 0], right[:, 1]) + mult(left[:, 1], right[:, 0])
    return jnp.stack([real_part, imag_part], axis=1)


def flipped(block):
    return jnp.swapaxes(block, -1, -2)


def herm(block):
    return jnp.stack([flipped(block[:, 0]), -flipped(block[:, 1])], axis=1)


def imtrace(left, right):
    return jnp.sum(
        left[:, 0] * flipped(right[:, 1]) + left[:, 1] * flipped(right[:, 0]), axis=(-2, -1)
    )


def compose(earlier, later):
    m_early, c_early = earlier
    m_late, c_late = later
    accum = cdot(cdot(m_late, c_early), herm(m_late)) + c_late
    return (cdot(m_late, m_early), accum)


def on_device(green, couplings, gamma, occupation, lead_occ, energy_weight):
    energies = green.shape[0]
    slab_count = green.shape[1]
    width = green.shape[-1]
    eye = jnp.eye(width, dtype=jnp.float32)
    zeros = jnp.zeros((width, width), jnp.float32)
    ident = jnp.stack([eye, zeros])[None]
    empty = jnp.zeros((energies, 2, width, width), jnp.float32)
    slab = 0
    block = green[:, slab]
    full = block.astype(jnp.float32)
    coupling = couplings[slab][None]
    blocks = [block]
    fblocks = [full]
    cblocks = [coupling]
    cfull = [coupling.astype(jnp.float32)]
    amaps = [cdot(block, coupling)]
    weighted = full * gamma[slab][None, None, None, :]
    sources = [occupation[:, slab][:, None, None, None] * cdot(weighted, herm(full))]
    fwd_m = amaps[0]
    fwd_c = sources[0]
    last = slab_count - 1
    bwd_m = cdot(herm(cblocks[last]), blocks[last])
    bwd_c = cdot(cdot(herm(cfull[last]), sources[last]), cfull[last])
    prefix_m, prefix_c = carried_in((fwd_m, fwd_c), "slab", compose, (ident, empty), False)
    suffix_m, suffix_c = carried_in((bwd_m, bwd_c), "slab", compose, (ident, empty), True)
    state = lead_occ[:, None, None, None] * cdot(prefix_m, herm(prefix_m)) + prefix_c
    slab = 0
    product = cdot(amaps[slab], state)
    flows = imtrace(product, herm(cfull[slab]))
    state = cdot(product, herm(amaps[slab])) + sources[slab]
    states = [state]
    backs = [None] * slab_count
    slab = 0
    full = fblocks[slab]
    backs[slab] = imtrace(full, suffix_c)
    currents = jnp.stack([jnp.sum(energy_weight * (flows - backs[0])) / width])
    return (jnp.stack(states, axis=1), currents)


def solution(mesh):
    return jax.shard_map(
        on_device,
        mesh=mesh,
        in_specs=(
            P("group", "slab", None, None, None),
            P("slab", None, None, None),
            P("slab", None),
            P("group", "slab"),
            P("group"),
            P("group"),
        ),
        out_specs=(P("group", "slab", None, None, None), P(("group", "slab"))),
        check_vma=False,
    )
```

profile of v0, /device:TPU:31, one launch (start us, length us, event | category | flops | bytes accessed | tf_op | source)
XLA Modules:
  0.0 419.3 jit_solution(9275309361033154679)
XLA Ops:
  7.2 1.1 copy.12
  12.8 1.1 fusion.105
  13.9 1.1 fusion.118
  15.1 1.1 convolution_add_fusion.12
  25.6 60.8 %all-gather.8.cloned.1.call-done = f32[16,1,2,256,256]{4,3,2,1,0:T(8,128)} async-done(((f32[1,1,2,256,256]{4,3,2,1,0:T(8,128)}), f32[16,1,2,256,256]{4,3,2,1,0:T(8,128)}) %all-gather.8.cloned.1.call-update) | async-done | bytes 8388624 | tf_op jit(solution)/shard_map/all_gather | solution.py:9
  86.5 75.9 %all-gather.10.cloned.1.call-done = f32[16,2,256,256]{3,2,1,0:T(8,128)} async-done(((f32[1,2,256,256]{3,2,1,0:T(8,128)}), f32[16,2,256,256]{3,2,1,0:T(8,128)}) %all-gather.10.cloned.1.call-update) | async-done | bytes 8388624 | tf_op jit(solution)/shard_map/all_gather | solution.py:9
  162.4 117.0 %while.32 = (s32[]{:T(128)}, f32[1,2,256,256]{3,2,1,0:T(8,128)S(1)}, f32[1,2,256,256]{3,2,1,0:T(8,128)S(1)}, s32[]{:T(128)}, f32[16,1,2,256,256]{4,3,2,1,0:T(8,1...) while((s32[]{:T(128)}, f32[1,2,256,256]{3,2,1,0:T(8,128)S(1)}, ...), condition=%wide.region_1.2_spmd.clone, body=%wide.region_0.1_spmd.clone.sunk | while | flops 2417360896 | bytes 16777328 | solution.py:22
  168.3 1.4 maximum_select_fusion.2
  175.6 1.4 maximum_select_fusion.2
  177.0 1.1 dynamic-slice_bitcast_fusion.4
  182.9 1.4 maximum_select_fusion.2
  190.2 1.4 maximum_select_fusion.2
  197.5 1.4 maximum_select_fusion.2
  198.9 1.2 dynamic-slice_bitcast_fusion.4
  204.9 1.4 maximum_select_fusion.2
  206.3 1.1 dynamic-slice_bitcast_fusion.4
  212.2 1.4 maximum_select_fusion.2
  219.5 1.4 maximum_select_fusion.2
  226.8 1.4 maximum_select_fusion.2
  228.2 1.2 dynamic-slice_bitcast_fusion.4
  234.2 1.4 maximum_select_fusion.2
  241.5 1.4 maximum_select_fusion.2
  248.8 1.4 maximum_select_fusion.2
  256.1 1.4 maximum_select_fusion.2
  257.5 1.1 dynamic-slice_bitcast_fusion.4
  263.4 1.4 maximum_select_fusion.2
  270.7 1.4 maximum_select_fusion.2
  278.0 1.4 maximum_select_fusion.2
  281.1 1.1 fusion.85
  282.6 1.4 convolution_subtract_fusion.9
  284.0 1.1 fusion.136
  285.1 1.1 fusion.67
  286.2 26.7 %all-gather.12.cloned.1.call-done = f32[16,2,256,256]{3,2,1,0:T(8,128)} async-done(((f32[1,2,256,256]{3,2,1,0:T(8,128)}), f32[16,2,256,256]{3,2,1,0:T(8,128)}) %all-gather.12.cloned.1.call-update) | async-done | bytes 8388624 | tf_op jit(solution)/shard_map/all_gather | solution.py:9
  312.9 89.9 %while.33 = (s32[]{:T(128)}, f32[1,2,256,256]{3,2,1,0:T(8,128)S(1)}, s32[]{:T(128)}, f32[16,1,2,256,256]{4,3,2,1,0:T(8,128)}, f32[16,1,2,256,256]{4,3,2,1,0:T(8,...) while((s32[]{:T(128)}, f32[1,2,256,256]{3,2,1,0:T(8,128)S(1)}, s32[]{:T(128)}, ...), condition=%wide.region_4.5_spmd.clone, body=%wide.region_3.4_spmd.clone.sunk | while | flops 1611661312 | bytes 11534504 | solution.py:22
  312.9 1.1 dynamic-slice_bitcast_fusion.5
  317.4 1.2 fusion.236
  318.6 1.1 dynamic-slice_bitcast_fusion.5
  323.0 1.2 fusion.236
  324.2 1.1 dynamic-slice_bitcast_fusion.5
  328.6 1.2 fusion.236
  329.8 1.1 dynamic-slice_bitcast_fusion.5
  334.2 1.2 fusion.236
  335.5 1.1 dynamic-slice_bitcast_fusion.5
  339.8 1.2 fusion.236
  341.1 1.1 dynamic-slice_bitcast_fusion.5
  345.4 1.2 fusion.236
  351.1 1.2 fusion.236
  356.7 1.2 fusion.236
  362.3 1.2 fusion.236
  367.9 1.2 fusion.236
  369.2 1.1 dynamic-slice_bitcast_fusion.5
  373.5 1.2 fusion.236
  374.8 1.1 dynamic-slice_bitcast_fusion.5
  379.1 1.2 fusion.236
  380.4 1.1 dynamic-slice_bitcast_fusion.5
  384.8 1.2 fusion.236
  386.0 1.1 dynamic-slice_bitcast_fusion.5
  390.4 1.2 fusion.236
  396.0 1.2 fusion.236
  401.6 1.2 fusion.236
  403.6 2.1 fusion.64
  405.7 1.4 fusion.55
  407.1 1.4 fusion.54
  409.7 1.9 maximum_add_fusion.2
  (430 shorter events, 159.8 us)
Async XLA Ops:
  7.2 9.0 %copy-start = (bf16[1,2,256,256]{3,2,1,0:T(8,128)(2,1)S(1)}, bf16[1,2,256,256]{3,2,1,0:T(8,128)(2,1)}, u32[]{:S(2)}) copy-start(bf16[1,2,256,256]{3,2,1,0:T(8,128)(2,1)} %param.11) | copy-start | bytes 786436
  7.2 79.3 %all-gather.8.cloned.1.call-start = ((), (), s32[]{:S(2)}) async-start(), calls=%async_computation | async-start | bytes 8912896 | tf_op jit(solution)/shard_map/all_gather | solution.py:9
  8.4 2.8 copy-start.3
  10.8 11.9 %copy-start.6 = (f32[256,256]{1,0:T(8,128)}, f32[256,256]{1,0:T(8,128)S(1)}, u32[]{:S(2)}) copy-start(f32[256,256]{1,0:T(8,128)S(1)} %convolution_subtract_fusion.11) | copy-start | bytes 786436
  11.2 11.7 %copy-start.5 = (f32[256,256]{1,0:T(8,128)}, f32[256,256]{1,0:T(8,128)S(1)}, u32[]{:S(2)}) copy-start(f32[256,256]{1,0:T(8,128)S(1)} %convolution_add_fusion.11) | copy-start | bytes 786436
  12.8 149.6 %all-gather.10.cloned.1.call-start = ((), (), s32[]{:S(2)}) async-start(), calls=%async_computation.1 | async-start | bytes 8912896 | tf_op jit(solution)/shard_map/all_gather | solution.py:9
  16.2 0.7 copy-start.1
  17.8 268.4 %all-gather.14.cloned.1.call-start = ((), (), s32[]{:S(2)}) async-start(), calls=%async_computation.3 | async-start | bytes 8912896 | tf_op jit(solution)/shard_map/all_gather | solution.py:9
  17.9 2.5 copy-start.7
  22.4 290.5 %all-gather.12.cloned.1.call-start = ((), (), s32[]{:S(2)}) async-start(), calls=%async_computation.2 | async-start | bytes 8912896 | tf_op jit(solution)/shard_map/all_gather | solution.py:9
  279.4 5.7 %copy-start.2 = (f32[256,256]{1,0:T(8,128)S(1)}, f32[256,256]{1,0:T(8,128)}, u32[]{:S(2)}) copy-start(f32[256,256]{1,0:T(8,128)} %copy-done.1) | copy-start | bytes 786436
  312.9 89.9 %copy-start.4 = (f32[1,2,256,256]{2,3,1,0:T(8,128)S(1)}, f32[1,2,256,256]{2,3,1,0:T(8,128)}, u32[]{:S(2)}) copy-start(f32[1,2,256,256]{2,3,1,0:T(8,128)} %copy-done.3) | copy-start | bytes 1572868
Sparse Core Ops, SparseCore 0:
  12.9 73.5 all-gather.7
  89.2 73.1 all-gather.9
  164.5 73.1 all-gather.13
  239.7 73.1 all-gather.11
where the time goes:
time: 427 us; the launch traced here: 419 us
  waiting for transfers between devices  164 us (38%)
  matrix products  147 us (34%)
  other arithmetic  49.4 us (12%)
  local copies, waits for them, and re-layouts  36.5 us (9%)
  between operations  18.5 us (4%)
    all_gather x4, waiting for transfers between devices, carried_in(): everything = jax.tree.map(lambda part: lax.all_gather(part, axis), array)  163 us
    dot_general x352, matrix products, mult(): jnp.einsum('eij,ejk->eik', left, right, preferred_element_type=jnp.float3...  147 us
    select_n x32, other arithmetic, hop(): return jax.tree.map(lambda a, b: jnp.where(reached, a, b), new, before)  41.2 us
    squeeze x32, local copies, waits for them, and re-layouts, hop(): new = combine(before, jax.tree.map(lambda part: part[at], everything))  34.9 us
  transfers between devices with their start and end apart: 4, of which 3 were waited for; matrix products, arithmetic and copies ran while one was open for 32% of the time, Pallas kernels for 0%

commit v1 on v0

v1 whole, which is shorter than its diff:
```python
import jax
import jax.numpy as jnp
from jax import lax
from jax.experimental import pallas as pl
from jax.experimental.pallas import tpu as pltpu
from jax.sharding import PartitionSpec as P

F32 = jnp.float32
BF16 = jnp.bfloat16
CHUNKS = 2


def split(value):
    high = value.astype(BF16)
    return high, (value - high.astype(F32)).astype(BF16)


def dot(left, right):
    return jnp.dot(left, right, preferred_element_type=F32)


def kernel(
    green,
    coupling,
    gamma,
    occupation,
    lead_occ,
    energy_weight,
    out,
    current,
    maps,
    sources,
    their_map,
    their_source,
    w_high,
    w_low,
    q_high,
    q_low,
    r_high,
    r_low,
    uv,
    total_source,
    chain_in,
    chain_out,
    mid_in,
    mid_out,
    trace_w,
    sums,
    swap_send,
    swap_recv,
    chain_send,
    chain_recv,
    mid_send,
    mid_recv,
):
    n = green.shape[-1]
    rows = n // CHUNKS
    count = lax.axis_size("slab")
    index = lax.axis_index("slab")
    core = lax.rem(index, 2)
    chip = lax.div(index, 2)
    chips = count // 2
    partner = index + 1 - 2 * core
    ahead = index + 2 - 4 * core
    place = chip + core * (chips - 1 - 2 * chip)
    last = chips - 1

    barrier = pltpu.get_barrier_semaphore()
    pl.semaphore_signal(barrier, inc=1, device_id={"slab": partner})

    @pl.when(chip > 0)
    def _():
        pl.semaphore_signal(barrier, inc=1, device_id={"slab": index - 2})

    @pl.when(chip < last)
    def _():
        pl.semaphore_signal(barrier, inc=1, device_id={"slab": index + 2})

    def prepare(slot, real, imag, exact=False):
        for part, w_ref, q_ref in ((0, w_high, q_high), (1, w_low, q_low)):
            if exact and part == 1:
                break
            a = split(real)[part]
            b = split(imag)[part]
            w_ref[slot, :n, :n] = a
            w_ref[slot, :n, n:] = b
            w_ref[slot, n:, :n] = b
            w_ref[slot, n:, n:] = -a
            q_ref[slot, :n] = a.astype(F32).T.astype(BF16)
            q_ref[slot, n:] = b.astype(F32).T.astype(BF16)

    def load(ref, chunk):
        at = slice(chunk * rows, (chunk + 1) * rows)
        high, low = split(ref[at, :])
        r_high[at, :] = high
        r_low[at, :] = low
        high, low = split(ref[at, :].T)
        r_high[n:, at] = high
        r_low[n:, at] = low

    def first(slot, exact=False):
        value = dot(w_high[slot], r_high[...]) + dot(w_high[slot], r_low[...])
        if not exact:
            value += dot(w_low[slot], r_high[...])
        uv[...] = value

    def second(slot, chunk, exact=False):
        total = None
        for side in range(2):
            at = slice(side * n + chunk * rows, side * n + (chunk + 1) * rows)
            high, low = split(uv[at, :])
            k = slice(side * n, (side + 1) * n)
            value = dot(high, q_high[slot, k]) + dot(low, q_high[slot, k])
            if not exact:
                value += dot(high, q_low[slot, k])
            total = value if total is None else total + value
        return total

    def chunk_rows(chunk):
        return slice(chunk * rows, (chunk + 1) * rows)

    def swap(which, source, target):
        return pltpu.make_async_remote_copy(
            src_ref=source,
            dst_ref=target,
            send_sem=swap_send.at[which],
            recv_sem=swap_recv.at[which],
            device_id={"slab": partner},
        )

    def chain_copy(chunk):
        return pltpu.make_async_remote_copy(
            src_ref=chain_out.at[pl.ds(chunk * rows, rows)],
            dst_ref=chain_in.at[pl.ds(chunk * rows, rows)],
            send_sem=chain_send.at[chunk],
            recv_sem=chain_recv.at[chunk],
            device_id={"slab": ahead},
        )

    def mid_copy(chunk):
        return pltpu.make_async_remote_copy(
            src_ref=mid_out.at[pl.ds(chunk * rows, rows)],
            dst_ref=mid_in.at[pl.ds(chunk * rows, rows)],
            send_sem=mid_send.at[chunk],
            recv_sem=mid_recv.at[chunk],
            device_id={"slab": partner},
        )

    g_r, g_i = green[0], green[1]
    c_r, c_i = coupling[0], coupling[1]
    maps[0, 0] = dot(g_r, c_r) - dot(g_i, c_i)
    maps[0, 1] = dot(g_r, c_i) + dot(g_i, c_r)
    ct_r = c_r.astype(F32).T.astype(BF16)
    ct_i = c_i.astype(F32).T.astype(BF16)
    maps[1, 0] = dot(ct_r, g_r) + dot(ct_i, g_i)
    maps[1, 1] = dot(ct_r, g_i) - dot(ct_i, g_r)

    pl.semaphore_wait(
        barrier, 1 + (chip > 0).astype(jnp.int32) + (chip < last).astype(jnp.int32)
    )
    swap_map = swap(0, maps.at[1 - core], their_map)
    swap_map.start()

    occ = occupation[0, 0]
    gamma_row = gamma[...] * occ
    f_r, f_i = g_r.astype(F32), g_i.astype(F32)
    uv[:n] = (f_r + f_i) * gamma_row
    uv[n:] = (f_i - f_r) * gamma_row
    q_high[3, :n] = f_r.T.astype(BF16)
    q_high[3, n:] = f_i.T.astype(BF16)
    for chunk in range(CHUNKS):
        sources[0, chunk_rows(chunk), :] = second(3, chunk, exact=True)
    trace_w[...] = 0.5 * ((f_i - f_r) + (f_i + f_r).T)
    prepare(3, ct_r.astype(F32), -ct_i.astype(F32), exact=True)
    for chunk in range(CHUNKS):
        load(sources.at[0], chunk)
    first(3, exact=True)
    for chunk in range(CHUNKS):
        sources[1, chunk_rows(chunk), :] = second(3, chunk, exact=True)
    swap_source = swap(1, sources.at[1 - core], their_source)
    swap_source.start()

    prepare(0, maps[core, 0], maps[core, 1])
    prepare(1, maps[1 - core, 0], maps[1 - core, 1])

    for chunk in range(CHUNKS):
        load(sources.at[core], chunk)
    swap_map.wait_recv()
    prepare(3, their_map[0], their_map[1])
    first(3)
    for chunk in range(CHUNKS):
        total_source[chunk_rows(chunk), :] = second(3, chunk)
    r_high[:n], r_low[:n] = split(maps[core, 0])
    r_high[n:], r_low[n:] = split(-maps[core, 1])
    uv[:n] = (
        dot(w_high[3, :n], r_high[...])
        + dot(w_high[3, :n], r_low[...])
        + dot(w_low[3, :n], r_high[...])
    )
    r_high[:n], r_low[:n] = split(maps[core, 1])
    r_high[n:], r_low[n:] = split(maps[core, 0])
    uv[n:] = (
        dot(w_high[3, :n], r_high[...])
        + dot(w_high[3, :n], r_low[...])
        + dot(w_low[3, :n], r_high[...])
    )
    prepare(2, uv[:n], uv[n:])
    swap_source.wait_recv()
    total_source[...] += their_source[...]

    def flow():
        weight_u = 0.5 * (coupling[0].astype(F32) - coupling[1].astype(F32))
        weight_v = 0.5 * (coupling[0].astype(F32) + coupling[1].astype(F32))
        sums[0] = jnp.sum(uv[:n] * weight_u + uv[n:] * weight_v)

    def back(ref):
        sums[1] = jnp.sum(ref[...] * trace_w[...])

    def emit(ref):
        block = ref[...]
        turned = block.T
        out[0] = 0.5 * (block + turned)
        out[1] = 0.5 * (block - turned)

    def chain():
        @pl.when(place == 0)
        def _():
            row = lax.broadcasted_iota(jnp.int32, (n, n), 0)
            column = lax.broadcasted_iota(jnp.int32, (n, n), 1)
            level = lead_occ[0] * (1 - core).astype(F32)
            chain_in[...] = jnp.where(row == column, level, 0.0)

        for chunk in range(CHUNKS):
            @pl.when(place > 0)
            def _():
                chain_copy(chunk).wait_recv()

            load(chain_in, chunk)

        @pl.when(place < last)
        def _():
            first(2)
            for chunk in range(CHUNKS):
                at = chunk_rows(chunk)
                chain_out[at, :] = second(2, chunk) + total_source[at, :]
                chain_copy(chunk).start()

        first(0)
        for chunk in range(CHUNKS):
            at = chunk_rows(chunk)
            mid_out[at, :] = second(0, chunk) + sources[core, at, :]
            mid_copy(chunk).start()

        @pl.when(core == 0)
        def _():
            flow()
            emit(mid_out)

        @pl.when(core == 1)
        def _():
            back(chain_in)

    def middle():
        for chunk in range(CHUNKS):
            mid_copy(chunk).wait_recv()

        @pl.when(core == 0)
        def _():
            back(mid_in)

        @pl.when(core == 1)
        def _():
            for chunk in range(CHUNKS):
                load(mid_in, chunk)
            first(1)
            for chunk in range(CHUNKS):
                at = chunk_rows(chunk)
                chain_spare[at, :] = second(1, chunk) + sources[0, at, :]
            flow()
            emit(chain_spare)

    chain_spare = their_source
    early = (place <= chips // 2).astype(jnp.int32)

    def phase(step, carry):
        @pl.when(step + early == 1)
        def _():
            chain()

        @pl.when(step + early != 1)
        def _():
            middle()

        return carry

    lax.fori_loop(0, 2, phase, 0)
    current[0] = energy_weight[0] * (sums[0] - sums[1]) / n

    swap_map.wait_send()
    swap_source.wait_send()
    for chunk in range(CHUNKS):
        mid_copy(chunk).wait_send()

        @pl.when(place < last)
        def _():
            chain_copy(chunk).wait_send()


def on_device(green, couplings, gamma, occupation, lead_occ, energy_weight):
    n = green.shape[-1]
    vmem = pl.BlockSpec(memory_space=pltpu.VMEM)
    smem = pl.BlockSpec(memory_space=pltpu.SMEM)
    block = lambda *lead: pltpu.VMEM((*lead, n, n), F32)
    wide = lambda *shape: pltpu.VMEM(shape, BF16)
    state, current = pl.pallas_call(
        kernel,
        out_shape=(
            jax.ShapeDtypeStruct((2, n, n), F32),
            jax.ShapeDtypeStruct((1,), F32),
        ),
        in_specs=[vmem, vmem, vmem, smem, smem, smem],
        out_specs=(vmem, smem),
        scratch_shapes=[
            block(2, 2),
            block(2),
            block(2),
            block(),
            wide(4, 2 * n, 2 * n),
            wide(4, 2 * n, 2 * n),
            wide(4, 2 * n, n),
            wide(4, 2 * n, n),
            wide(2 * n, n),
            wide(2 * n, n),
            pltpu.VMEM((2 * n, n), F32),
            block(),
            block(),
            block(),
            block(),
            block(),
            block(),
            pltpu.SMEM((2,), F32),
            pltpu.SemaphoreType.DMA((2,)),
            pltpu.SemaphoreType.DMA((2,)),
            pltpu.SemaphoreType.DMA((CHUNKS,)),
            pltpu.SemaphoreType.DMA((CHUNKS,)),
            pltpu.SemaphoreType.DMA((CHUNKS,)),
            pltpu.SemaphoreType.DMA((CHUNKS,)),
        ],
        compiler_params=pltpu.CompilerParams(
            collective_id=0, has_side_effects=True, vmem_limit_bytes=40 * 2**20
        ),
    )(
        green.reshape(2, n, n),
        couplings.reshape(2, n, n),
        gamma,
        occupation,
        lead_occ,
        energy_weight,
    )
    return state.reshape(1, 1, 2, n, n), current


def solution(mesh):
    return jax.shard_map(
        on_device,
        mesh=mesh,
        in_specs=(
            P("group", "slab", None, None, None),
            P("slab", None, None, None),
            P("slab", None),
            P("group", "slab"),
            P("group"),
            P("group"),
        ),
        out_specs=(P("group", "slab", None, None, None), P(("group", "slab"))),
        check_vma=False,
    )
```

time: 427 us -> 62.5 us (0.15); the launches traced: 419 us -> 62.3 us
  waiting for transfers between devices: 164 us -> 0 us
  matrix products: 147 us -> 0 us
  Pallas kernels: 0 us -> 54.6 us
  other arithmetic: 49.4 us -> 0 us
  local copies, waits for them, and re-layouts: 36.5 us -> 3.37 us
  between operations: 18.5 us -> 4.32 us
    all_gather x4 -> x0, waiting for transfers between devices: 163 us -> none  [carried_in(): everything = jax.tree.map(lambda part: lax.all_gather(part, axis), array)]
    dot_general x352 -> x0, matrix products: 147 us -> none  [mult(): jnp.einsum('eij,ejk->eik', left, right, preferred_element_type=jnp.float3...]
    pallas_call x0 -> x1, Pallas kernels: none -> 54.6 us  [on_device(): pl.pallas_call(kernel, out_shape=(jax.ShapeDtypeStruct((2, n, n), F32), j...]
    select_n x32 -> x0, other arithmetic: 41.2 us -> none  [hop(): return jax.tree.map(lambda a, b: jnp.where(reached, a, b), new, before)]
    squeeze x32 -> x0, local copies, waits for them, and re-layouts: 34.9 us -> none  [hop(): new = combine(before, jax.tree.map(lambda part: part[at], everything))]
  transfers between devices with their start and end apart: 4 -> 0, of which waited for: 3 -> 0; matrix products, arithmetic and copies ran while one was open for 32% -> 0% of each run, Pallas kernels for 0% -> 0%
where the time goes in v1:
time: 62.5 us; the launch traced here: 62.3 us
  Pallas kernels  54.6 us (87%)
  between operations  4.32 us (7%)
  local copies, waits for them, and re-layouts  3.37 us (5%)
    pallas_call x1, Pallas kernels, on_device(): pl.pallas_call(kernel, out_shape=(jax.ShapeDtypeStruct((2, n, n), F32), j...  54.6 us
    unnamed x7, local copies, waits for them, and re-layouts  3.37 us

profile of v1, /device:TPU:31, one launch (start us, length us, event | category | flops | bytes accessed | tf_op | source)
XLA Modules:
  0.0 62.3 jit_solution(5182606996692992406)
XLA Ops:
  2.6 0.0 copy-start.2
  2.6 0.7 %copy-done.2 = f32[1,256]{1,0:T(1,128)S(1)} copy-done((f32[1,256]{1,0:T(1,128)S(1)}, f32[1,256]{1,0:T(1,128)}, u32[]{:S(2)}) %copy-start.2) | copy-done | bytes 1048
  3.2 0.0 copy-start
  3.2 0.9 %copy-done = bf16[1,1,2,256,256]{4,3,2,1,0:T(8,128)(2,1)S(1)} copy-done((bf16[1,1,2,256,256]{4,3,2,1,0:T(8,128)(2,1)S(1)}, bf16[1,1,2,256,256]{4,3,2,1,0:T(8,128)(2,1)}, u32[]{:S(2)}) %copy-start) | copy-done | bytes 262168
  4.2 0.0 copy-start.1
  4.2 0.9 %copy-done.1 = bf16[1,2,256,256]{3,2,1,0:T(8,128)(2,1)S(1)} copy-done((bf16[1,2,256,256]{3,2,1,0:T(8,128)(2,1)S(1)}, bf16[1,2,256,256]{3,2,1,0:T(8,128)(2,1)}, u32[]{:S(2)}) %copy-start.1) | copy-done | bytes 262168
  5.1 54.6 %shard_map.77 = (f32[2,256,256]{2,1,0:T(8,128)S(1)}, f32[1]{0:T(128)}) custom-call(bf16[2,256,256]{2,1,0:T(8,128)(2,1)S(1)} %bitcast.4, bf16[2,256,256]{2,1,0:T(8,128)(2,1)S(1)} %bitcast.5, f32[1,256]{1,0:T(1,128)S(1)} %copy-done.2, f32[1,1]{1,0:T(1,128)S(6)} %copy.10.occupation, f32[1]{0:T(128)S(6)} %copy.11.lead_occ, f32[1]{0:T(128)S(6)} %copy.12.energy_weight), custom_call_target="tpu_custom_call" | custom-call | tf_op jit(solution)/shard_map/pallas_call | solution.py:315
  59.7 0.8 %copy.13 = f32[1,1,2,256,256]{4,3,2,1,0:T(8,128)} copy(f32[1,1,2,256,256]{4,3,2,1,0:T(8,128)S(1)} %bitcast.3) | data formatting | bytes 1048576
Async XLA Ops:
  2.6 0.7 %copy-start.2 = (f32[1,256]{1,0:T(1,128)S(1)}, f32[1,256]{1,0:T(1,128)}, u32[]{:S(2)}) copy-start(f32[1,256]{1,0:T(1,128)} %gamma.1) | copy-start | bytes 3076
  3.2 0.9 %copy-start = (bf16[1,1,2,256,256]{4,3,2,1,0:T(8,128)(2,1)S(1)}, bf16[1,1,2,256,256]{4,3,2,1,0:T(8,128)(2,1)}, u32[]{:S(2)}) copy-start(bf16[1,1,2,256,256]{4,3,2,1,0:T(8,128)(2,1)} %param.6) | copy-start | bytes 786436
  4.2 0.9 %copy-start.1 = (bf16[1,2,256,256]{3,2,1,0:T(8,128)(2,1)S(1)}, bf16[1,2,256,256]{3,2,1,0:T(8,128)(2,1)}, u32[]{:S(2)}) copy-start(bf16[1,2,256,256]{3,2,1,0:T(8,128)(2,1)} %param.7) | copy-start | bytes 786436

commit v2 on v1

--- a/solution.py
+++ b/solution.py
@@ -20,14 +20,18 @@
 
 
 def kernel(
-    green,
-    coupling,
-    gamma,
+    green_in,
+    coupling_in,
+    gamma_in,
     occupation,
     lead_occ,
     energy_weight,
     out,
     current,
+    green,
+    coupling,
+    gamma,
+    fetched,
     maps,
     sources,
     their_map,
@@ -39,7 +43,13 @@
     r_high,
     r_low,
     uv,
-    total_source,
+    pair_map,
+    pair_source,
+    head_out,
+    head_map,
+    head_source,
+    quad_source,
+    state_in,
     chain_in,
     chain_out,
     mid_in,
@@ -48,6 +58,8 @@
     sums,
     swap_send,
     swap_recv,
+    head_send,
+    head_recv,
     chain_send,
     chain_recv,
     mid_send,
@@ -60,21 +72,39 @@
     core = lax.rem(index, 2)
     chip = lax.div(index, 2)
     chips = count // 2
-    partner = index + 1 - 2 * core
-    ahead = index + 2 - 4 * core
-    place = chip + core * (chips - 1 - 2 * chip)
-    last = chips - 1
+    quads = count // 4
+    sign = 1 - 2 * core
+    partner = index + sign
+    next_near = index + 2 * sign
+    next_far = index + 4 * sign
+    tail = lax.rem(chip + core, 2)
+    quad = lax.div(chip, 2)
+    place = quad + core * (quads - 1 - 2 * quad)
+    last = quads - 1
+
+    fetches = [
+        pltpu.make_async_copy(source, target, fetched.at[at])
+        for at, (source, target) in enumerate(
+            ((green_in, green), (coupling_in, coupling), (gamma_in, gamma))
+        )
+    ]
+    for fetch in fetches:
+        fetch.start()
 
     barrier = pltpu.get_barrier_semaphore()
     pl.semaphore_signal(barrier, inc=1, device_id={"slab": partner})
-
-    @pl.when(chip > 0)
-    def _():
-        pl.semaphore_signal(barrier, inc=1, device_id={"slab": index - 2})
-
-    @pl.when(chip < last)
-    def _():
-        pl.semaphore_signal(barrier, inc=1, device_id={"slab": index + 2})
+    greeted = 1
+    for step in (-4, -2, 2, 4):
+        there = index + step
+        inside = jnp.logical_and(there >= 0, there < count)
+        greeted = greeted + inside.astype(jnp.int32)
+
+        @pl.when(inside)
+        def _():
+            pl.semaphore_signal(barrier, inc=1, device_id={"slab": there})
+
+    for fetch in fetches:
+        fetch.wait()
 
     def prepare(slot, real, imag, exact=False):
         for part, w_ref, q_ref in ((0, w_high, q_high), (1, w_low, q_low)):
@@ -128,13 +158,22 @@
             device_id={"slab": partner},
         )
 
-    def chain_copy(chunk):
+    def chain_copy(chunk, which):
         return pltpu.make_async_remote_copy(
             src_ref=chain_out.at[pl.ds(chunk * rows, rows)],
             dst_ref=chain_in.at[pl.ds(chunk * rows, rows)],
-            send_sem=chain_send.at[chunk],
+            send_sem=chain_send.at[which, chunk],
             recv_sem=chain_recv.at[chunk],
-            device_id={"slab": ahead},
+            device_id={"slab": (next_far, next_near)[which]},
+        )
+
+    def head_copy(which, source, target):
+        return pltpu.make_async_remote_copy(
+            src_ref=source,
+            dst_ref=target,
+            send_sem=head_send.at[which],
+            recv_sem=head_recv.at[which],
+            device_id={"slab": next_near},
         )
 
     def mid_copy(chunk):
@@ -155,9 +194,7 @@
     maps[1, 0] = dot(ct_r, g_r) + dot(ct_i, g_i)
     maps[1, 1] = dot(ct_r, g_i) - dot(ct_i, g_r)
 
-    pl.semaphore_wait(
-        barrier, 1 + (chip > 0).astype(jnp.int32) + (chip < last).astype(jnp.int32)
-    )
+    pl.semaphore_wait(barrier, greeted)
     swap_map = swap(0, maps.at[1 - core], their_map)
     swap_map.start()
 
@@ -180,33 +217,56 @@
     swap_source = swap(1, sources.at[1 - core], their_source)
     swap_source.start()
 
-    prepare(0, maps[core, 0], maps[core, 1])
-    prepare(1, maps[1 - core, 0], maps[1 - core, 1])
+    def multiply(slot, ref):
+        real, imag = split(ref[0]), split(ref[1])
+        r_high[:n], r_low[:n] = real
+        r_high[n:], r_low[n:] = -imag[0], -imag[1]
+        for side in range(2):
+            if side == 1:
+                r_high[:n], r_low[:n] = imag
+                r_high[n:], r_low[n:] = real
+            uv[side * n : (side + 1) * n] = (
+                dot(w_high[slot, :n], r_high[...])
+                + dot(w_high[slot, :n], r_low[...])
+                + dot(w_low[slot, :n], r_high[...])
+            )
+
+    head_map_copy = head_copy(0, pair_map, head_map)
+    head_source_copy = head_copy(1, head_out, head_source)
+    sends_map = jnp.logical_and(tail == 0, place > 0)
+    swap_map.wait_recv()
+    prepare(3, their_map[0], their_map[1])
+    own = maps.at[core]
+    multiply(3, own)
+    pair_map[0] = uv[:n]
+    pair_map[1] = uv[n:]
+
+    @pl.when(sends_map)
+    def _():
+        head_map_copy.start()
 
     for chunk in range(CHUNKS):
         load(sources.at[core], chunk)
-    swap_map.wait_recv()
-    prepare(3, their_map[0], their_map[1])
     first(3)
+    swap_source.wait_recv()
     for chunk in range(CHUNKS):
-        total_source[chunk_rows(chunk), :] = second(3, chunk)
-    r_high[:n], r_low[:n] = split(maps[core, 0])
-    r_high[n:], r_low[n:] = split(-maps[core, 1])
-    uv[:n] = (
-        dot(w_high[3, :n], r_high[...])
-        + dot(w_high[3, :n], r_low[...])
-        + dot(w_low[3, :n], r_high[...])
-    )
-    r_high[:n], r_low[:n] = split(maps[core, 1])
-    r_high[n:], r_low[n:] = split(maps[core, 0])
-    uv[n:] = (
-        dot(w_high[3, :n], r_high[...])
-        + dot(w_high[3, :n], r_low[...])
-        + dot(w_low[3, :n], r_high[...])
-    )
-    prepare(2, uv[:n], uv[n:])
-    swap_source.wait_recv()
-    total_source[...] += their_source[...]
+        at = chunk_rows(chunk)
+        pair_source[at, :] = second(3, chunk) + their_source[at, :]
+
+    @pl.when(sends_map)
+    def _():
+        head_out[...] = pair_source[...]
+        head_source_copy.start()
+
+    @pl.when(jnp.logical_or(tail == 1, place == 0))
+    def _():
+        prepare(2, pair_map[0], pair_map[1])
+
+    prepare(0, maps[core, 0], maps[core, 1])
+
+    @pl.when(core == 1)
+    def _():
+        prepare(1, maps[0, 0], maps[0, 1])
 
     def flow():
         weight_u = 0.5 * (coupling[0].astype(F32) - coupling[1].astype(F32))
@@ -222,28 +282,92 @@
         out[0] = 0.5 * (block + turned)
         out[1] = 0.5 * (block - turned)
 
+    def relay(slot, source):
+        for chunk in range(CHUNKS):
+            at = chunk_rows(chunk)
+            chain_out[at, :] = second(slot, chunk) + source[at, :]
+
+            @pl.when(place < last)
+            def _():
+                chain_copy(chunk, 0).start()
+
+        @pl.when(place < last)
+        def _():
+            for chunk in range(CHUNKS):
+                chain_copy(chunk, 1).start()
+
+    def receive():
+        for chunk in range(CHUNKS):
+            chain_copy(chunk, 0).wait_recv()
+            load(chain_in, chunk)
+
     def chain():
-        @pl.when(place == 0)
-        def _():
-            row = lax.broadcasted_iota(jnp.int32, (n, n), 0)
-            column = lax.broadcasted_iota(jnp.int32, (n, n), 1)
-            level = lead_occ[0] * (1 - core).astype(F32)
-            chain_in[...] = jnp.where(row == column, level, 0.0)
-
-        for chunk in range(CHUNKS):
+        @pl.when(tail == 0)
+        def _():
+            @pl.when(place == 0)
+            def _():
+                row = lax.broadcasted_iota(jnp.int32, (n, n), 0)
+                column = lax.broadcasted_iota(jnp.int32, (n, n), 1)
+                level = lead_occ[0] * (1 - core).astype(F32)
+                chain_in[...] = jnp.where(row == column, level, 0.0)
+                for chunk in range(CHUNKS):
+                    load(chain_in, chunk)
+                first(2)
+                for chunk in range(CHUNKS):
+                    at = chunk_rows(chunk)
+                    head_out[at, :] = second(2, chunk) + pair_source[at, :]
+                head_source_copy.start()
+
             @pl.when(place > 0)
             def _():
-                chain_copy(chunk).wait_recv()
-
-            load(chain_in, chunk)
-
-        @pl.when(place < last)
-        def _():
-            first(2)
+                receive()
+
+            state_in[...] = chain_in[...]
+
+        @pl.when(tail == 1)
+        def _():
+            @pl.when(place > 0)
+            def _():
+                head_map_copy.wait_recv()
+                prepare(3, head_map[0], head_map[1])
+                multiply(2, head_map)
+                prepare(4, uv[:n], uv[n:])
+
+            head_source_copy.wait_recv()
+
+            @pl.when(jnp.logical_or(place == 0, place < last))
+            def _():
+                for chunk in range(CHUNKS):
+                    load(head_source, chunk)
+                first(2)
+
+            @pl.when(place == 0)
+            def _():
+                relay(2, pair_source)
+                state_in[...] = head_source[...]
+
+            @pl.when(place > 0)
+            def _():
+                @pl.when(place < last)
+                def _():
+                    for chunk in range(CHUNKS):
+                        at = chunk_rows(chunk)
+                        quad_source[at, :] = second(2, chunk) + pair_source[at, :]
+
+                receive()
+
+                @pl.when(place < last)
+                def _():
+                    first(4)
+                    relay(4, quad_source)
+
+                first(3)
+                for chunk in range(CHUNKS):
+                    at = chunk_rows(chunk)
+                    state_in[at, :] = second(3, chunk) + head_source[at, :]
+
             for chunk in range(CHUNKS):
-                at = chunk_rows(chunk)
-                chain_out[at, :] = second(2, chunk) + total_source[at, :]
-                chain_copy(chunk).start()
+                load(state_in, chunk)
 
         first(0)
         for chunk in range(CHUNKS):
@@ -258,7 +382,7 @@
 
         @pl.when(core == 1)
         def _():
-            back(chain_in)
+            back(state_in)
 
     def middle():
         for chunk in range(CHUNKS):
@@ -280,7 +404,7 @@
             emit(chain_spare)
 
     chain_spare = their_source
-    early = (place <= chips // 2).astype(jnp.int32)
+    early = (place <= quads // 2).astype(jnp.int32)
 
     def phase(step, carry):
         @pl.when(step + early == 1)
@@ -301,14 +425,25 @@
     for chunk in range(CHUNKS):
         mid_copy(chunk).wait_send()
 
-        @pl.when(place < last)
-        def _():
-            chain_copy(chunk).wait_send()
+    @pl.when(tail == 0)
+    def _():
+        head_source_copy.wait_send()
+
+        @pl.when(place > 0)
+        def _():
+            head_map_copy.wait_send()
+
+    @pl.when(jnp.logical_and(tail == 1, place < last))
+    def _():
+        for which in range(2):
+            for chunk in range(CHUNKS):
+                chain_copy(chunk, which).wait_send()
 
 
 def on_device(green, couplings, gamma, occupation, lead_occ, energy_weight):
     n = green.shape[-1]
     vmem = pl.BlockSpec(memory_space=pltpu.VMEM)
+    hbm = pl.BlockSpec(memory_space=pl.ANY)
     smem = pl.BlockSpec(memory_space=pltpu.SMEM)
     block = lambda *lead: pltpu.VMEM((*lead, n, n), F32)
     wide = lambda *shape: pltpu.VMEM(shape, BF16)
@@ -318,20 +453,30 @@
             jax.ShapeDtypeStruct((2, n, n), F32),
             jax.ShapeDtypeStruct((1,), F32),
         ),
-        in_specs=[vmem, vmem, vmem, smem, smem, smem],
+        in_specs=[hbm, hbm, hbm, smem, smem, smem],
         out_specs=(vmem, smem),
         scratch_shapes=[
+            wide(2, n, n),
+            wide(2, n, n),
+            pltpu.VMEM((1, n), F32),
+            pltpu.SemaphoreType.DMA((3,)),
             block(2, 2),
             block(2),
             block(2),
             block(),
-            wide(4, 2 * n, 2 * n),
-            wide(4, 2 * n, 2 * n),
-            wide(4, 2 * n, n),
-            wide(4, 2 * n, n),
+            wide(5, 2 * n, 2 * n),
+            wide(5, 2 * n, 2 * n),
+            wide(5, 2 * n, n),
+            wide(5, 2 * n, n),
             wide(2 * n, n),
             wide(2 * n, n),
             pltpu.VMEM((2 * n, n), F32),
+            block(2),
+            block(),
+            block(),
+            block(2),
+            block(),
+            block(),
             block(),
             block(),
             block(),
@@ -341,7 +486,9 @@
             pltpu.SMEM((2,), F32),
             pltpu.SemaphoreType.DMA((2,)),
             pltpu.SemaphoreType.DMA((2,)),
-            pltpu.SemaphoreType.DMA((CHUNKS,)),
+            pltpu.SemaphoreType.DMA((2,)),
+            pltpu.SemaphoreType.DMA((2,)),
+            pltpu.SemaphoreType.DMA((2, CHUNKS)),
             pltpu.SemaphoreType.DMA((CHUNKS,)),
             pltpu.SemaphoreType.DMA((CHUNKS,)),
             pltpu.SemaphoreType.DMA((CHUNKS,)),

time: 62.5 us -> 46.2 us (0.74)
  the two profiles are of different devices: /device:TPU:31 before, /device:TPU:27 now
where the time goes in v2:
time: 46.2 us; the launch traced here: 46 us
  Pallas kernels  38.3 us (83%)
  between operations  4.32 us (9%)
  local copies, waits for them, and re-layouts  3.37 us (7%)
    pallas_call x1, Pallas kernels, on_device(): pl.pallas_call(kernel, out_shape=(jax.ShapeDtypeStruct((2, n, n), F32), j...  38.3 us
    unnamed x7, local copies, waits for them, and re-layouts  3.37 us

profile of v2, /device:TPU:27, one launch (start us, length us, event | category | flops | bytes accessed | tf_op | source)
XLA Modules:
  0.0 46.0 jit_solution(1469616152014612385)
XLA Ops:
  2.6 0.0 copy-start.2
  2.6 0.7 %copy-done.2 = f32[1,256]{1,0:T(1,128)S(1)} copy-done((f32[1,256]{1,0:T(1,128)S(1)}, f32[1,256]{1,0:T(1,128)}, u32[]{:S(2)}) %copy-start.2) | copy-done | bytes 1048
  3.2 0.0 copy-start
  3.2 0.9 %copy-done = bf16[1,1,2,256,256]{4,3,2,1,0:T(8,128)(2,1)S(1)} copy-done((bf16[1,1,2,256,256]{4,3,2,1,0:T(8,128)(2,1)S(1)}, bf16[1,1,2,256,256]{4,3,2,1,0:T(8,128)(2,1)}, u32[]{:S(2)}) %copy-start) | copy-done | bytes 262168
  4.2 0.0 copy-start.1
  4.2 0.9 %copy-done.1 = bf16[1,2,256,256]{3,2,1,0:T(8,128)(2,1)S(1)} copy-done((bf16[1,2,256,256]{3,2,1,0:T(8,128)(2,1)S(1)}, bf16[1,2,256,256]{3,2,1,0:T(8,128)(2,1)}, u32[]{:S(2)}) %copy-start.1) | copy-done | bytes 262168
  5.1 38.3 %shard_map.77 = (f32[2,256,256]{2,1,0:T(8,128)S(1)}, f32[1]{0:T(128)}) custom-call(bf16[2,256,256]{2,1,0:T(8,128)(2,1)S(1)} %bitcast.4, bf16[2,256,256]{2,1,0:T(8,128)(2,1)S(1)} %bitcast.5, f32[1,256]{1,0:T(1,128)S(1)} %copy-done.2, f32[1,1]{1,0:T(1,128)S(6)} %copy.10.occupation, f32[1]{0:T(128)S(6)} %copy.11.lead_occ, f32[1]{0:T(128)S(6)} %copy.12.energy_weight), custom_call_target="tpu_custom_call" | custom-call | tf_op jit(solution)/shard_map/pallas_call | solution.py:450
  43.4 0.8 %copy.13 = f32[1,1,2,256,256]{4,3,2,1,0:T(8,128)} copy(f32[1,1,2,256,256]{4,3,2,1,0:T(8,128)S(1)} %bitcast.3) | data formatting | bytes 1048576
Async XLA Ops:
  2.6 0.7 %copy-start.2 = (f32[1,256]{1,0:T(1,128)S(1)}, f32[1,256]{1,0:T(1,128)}, u32[]{:S(2)}) copy-start(f32[1,256]{1,0:T(1,128)} %gamma_in.1) | copy-start | bytes 3076
  3.2 0.9 %copy-start = (bf16[1,1,2,256,256]{4,3,2,1,0:T(8,128)(2,1)S(1)}, bf16[1,1,2,256,256]{4,3,2,1,0:T(8,128)(2,1)}, u32[]{:S(2)}) copy-start(bf16[1,1,2,256,256]{4,3,2,1,0:T(8,128)(2,1)} %param.6) | copy-start | bytes 786436
  4.2 0.9 %copy-start.1 = (bf16[1,2,256,256]{3,2,1,0:T(8,128)(2,1)S(1)}, bf16[1,2,256,256]{3,2,1,0:T(8,128)(2,1)}, u32[]{:S(2)}) copy-start(bf16[1,2,256,256]{3,2,1,0:T(8,128)(2,1)} %param.7) | copy-start | bytes 786436

commit v3 on v2

--- a/solution.py
+++ b/solution.py
@@ -287,20 +287,37 @@
             at = chunk_rows(chunk)
             chain_out[at, :] = second(slot, chunk) + source[at, :]
 
-            @pl.when(place < last)
+            @pl.when(place < last - 1)
             def _():
                 chain_copy(chunk, 0).start()
 
-        @pl.when(place < last)
-        def _():
-            for chunk in range(CHUNKS):
+            @pl.when(place == last - 1)
+            def _():
                 chain_copy(chunk, 1).start()
+
+        for chunk in range(CHUNKS):
+            @pl.when(place < last - 1)
+            def _():
+                chain_copy(chunk, 1).start()
+
+            @pl.when(place == last - 1)
+            def _():
+                chain_copy(chunk, 0).start()
 
     def receive():
         for chunk in range(CHUNKS):
             chain_copy(chunk, 0).wait_recv()
             load(chain_in, chunk)
 
+    ends = jnp.logical_and(tail == 1, jnp.logical_and(place == last, place > 0))
+    base = 2 - 2 * ends.astype(jnp.int32)
+
+    def hand_over(slot, source):
+        for chunk in range(CHUNKS):
+            at = chunk_rows(chunk)
+            mid_out[at, :] = second(slot, chunk) + source[at, :]
+            mid_copy(chunk).start()
+
     def chain():
         @pl.when(tail == 0)
         def _():
@@ -310,13 +327,14 @@
                 column = lax.broadcasted_iota(jnp.int32, (n, n), 1)
                 level = lead_occ[0] * (1 - core).astype(F32)
                 chain_in[...] = jnp.where(row == column, level, 0.0)
-                for chunk in range(CHUNKS):
-                    load(chain_in, chunk)
-                first(2)
+                uv[:n] = level * (pair_map[0] + pair_map[1])
+                uv[n:] = level * (pair_map[1] - pair_map[0])
                 for chunk in range(CHUNKS):
                     at = chunk_rows(chunk)
                     head_out[at, :] = second(2, chunk) + pair_source[at, :]
                 head_source_copy.start()
+                for chunk in range(CHUNKS):
+                    load(chain_in, chunk)
 
             @pl.when(place > 0)
             def _():
@@ -330,16 +348,13 @@
             def _():
                 head_map_copy.wait_recv()
                 prepare(3, head_map[0], head_map[1])
-                multiply(2, head_map)
+                multiply(base, head_map)
                 prepare(4, uv[:n], uv[n:])
 
             head_source_copy.wait_recv()
-
-            @pl.when(jnp.logical_or(place == 0, place < last))
-            def _():
-                for chunk in range(CHUNKS):
-                    load(head_source, chunk)
-                first(2)
+            for chunk in range(CHUNKS):
+                load(head_source, chunk)
+            first(base)
 
             @pl.when(place == 0)
             def _():
@@ -348,18 +363,21 @@
 
             @pl.when(place > 0)
             def _():
-                @pl.when(place < last)
+                for chunk in range(CHUNKS):
+                    at = chunk_rows(chunk)
+                    quad_source[at, :] = second(base, chunk) + jnp.where(
+                        ends, sources[core, at, :], pair_source[at, :]
+                    )
+                receive()
+                first(4)
+
+                @pl.when(jnp.logical_not(ends))
                 def _():
-                    for chunk in range(CHUNKS):
-                        at = chunk_rows(chunk)
-                        quad_source[at, :] = second(2, chunk) + pair_source[at, :]
-
-                receive()
-
-                @pl.when(place < last)
+                    relay(4, quad_source)
+
+                @pl.when(ends)
                 def _():
-                    first(4)
-                    relay(4, quad_source)
+                    hand_over(4, quad_source)
 
                 first(3)
                 for chunk in range(CHUNKS):
@@ -370,10 +388,10 @@
                 load(state_in, chunk)
 
         first(0)
-        for chunk in range(CHUNKS):
-            at = chunk_rows(chunk)
-            mid_out[at, :] = second(0, chunk) + sources[core, at, :]
-            mid_copy(chunk).start()
+
+        @pl.when(jnp.logical_not(ends))
+        def _():
+            hand_over(0, sources.at[core])
 
         @pl.when(core == 0)
         def _():
@@ -494,7 +512,7 @@
             pltpu.SemaphoreType.DMA((CHUNKS,)),
         ],
         compiler_params=pltpu.CompilerParams(
-            collective_id=0, has_side_effects=True, vmem_limit_bytes=40 * 2**20
+            collective_id=0, has_side_effects=True, vmem_limit_bytes=62 * 2**20
         ),
     )(
         green.reshape(2, n, n),

time: 46.2 us -> 44.6 us (0.965)
  the two profiles are of different devices: /device:TPU:27 before, /device:TPU:1 now
where the time goes in v3:
time: 44.6 us; the launch traced here: 44.4 us
  Pallas kernels  38.3 us (86%)
  between operations  4.27 us (10%)
  local copies, waits for them, and re-layouts  1.87 us (4%)
    pallas_call x1, Pallas kernels, on_device(): pl.pallas_call(kernel, out_shape=(jax.ShapeDtypeStruct((2, n, n), F32), j...  38.3 us
    unnamed x1, local copies, waits for them, and re-layouts  1.87 us

profile of v3, /device:TPU:1, one launch (start us, length us, event | category | flops | bytes accessed | tf_op | source)
XLA Modules:
  0.0 44.4 jit_solution(4103688906582260098)
XLA Ops:
  2.6 38.3 %shard_map.77 = (f32[2,256,256]{2,1,0:T(8,128)}, f32[1]{0:T(128)}) custom-call(bf16[2,256,256]{2,1,0:T(8,128)(2,1)} %bitcast.4, bf16[2,256,256]{2,1,0:T(8,128)(2,1)} %bitcast.5, f32[1,256]{1,0:T(1,128)} %gamma_in.1, f32[1,1]{1,0:T(1,128)S(6)} %copy.10.occupation, f32[1]{0:T(128)S(6)} %copy.11.lead_occ, f32[1]{0:T(128)S(6)} %copy.12.energy_weight), custom_call_target="tpu_custom_call" | custom-call | tf_op jit(solution)/shard_map/pallas_call | solution.py:468
  40.8 1.9 %copy.13 = f32[1,1,2,256,256]{4,3,2,1,0:T(8,128)} copy(f32[1,1,2,256,256]{4,3,2,1,0:T(8,128)} %bitcast.3) | data formatting | bytes 1048576

commit v4 on v3

--- a/solution.py
+++ b/solution.py
@@ -198,24 +198,42 @@
     swap_map = swap(0, maps.at[1 - core], their_map)
     swap_map.start()
 
-    occ = occupation[0, 0]
-    gamma_row = gamma[...] * occ
-    f_r, f_i = g_r.astype(F32), g_i.astype(F32)
-    uv[:n] = (f_r + f_i) * gamma_row
-    uv[n:] = (f_i - f_r) * gamma_row
-    q_high[3, :n] = f_r.T.astype(BF16)
-    q_high[3, n:] = f_i.T.astype(BF16)
-    for chunk in range(CHUNKS):
-        sources[0, chunk_rows(chunk), :] = second(3, chunk, exact=True)
-    trace_w[...] = 0.5 * ((f_i - f_r) + (f_i + f_r).T)
-    prepare(3, ct_r.astype(F32), -ct_i.astype(F32), exact=True)
-    for chunk in range(CHUNKS):
-        load(sources.at[0], chunk)
-    first(3, exact=True)
-    for chunk in range(CHUNKS):
-        sources[1, chunk_rows(chunk), :] = second(3, chunk, exact=True)
+    gamma_row = gamma[...] * occupation[0, 0]
+
+    def source(which):
+        real, imag = (
+            (maps[1, 0], maps[1, 1])
+            if which
+            else (green[0].astype(F32), green[1].astype(F32))
+        )
+        uv[:n] = (real + imag) * gamma_row
+        uv[n:] = (imag - real) * gamma_row
+        for part, q_ref in ((0, q_high), (1, q_low))[: 1 + which]:
+            q_ref[4, :n] = split(real)[part].astype(F32).T.astype(BF16)
+            q_ref[4, n:] = split(imag)[part].astype(F32).T.astype(BF16)
+        for chunk in range(CHUNKS):
+            sources[which, chunk_rows(chunk), :] = second(4, chunk, exact=not which)
+
     swap_source = swap(1, sources.at[1 - core], their_source)
-    swap_source.start()
+    for mine in range(2):
+        @pl.when(core == mine)
+        def _():
+            source(1 - mine)
+            swap_source.start()
+            source(mine)
+
+    def trace_weights():
+        f_r, f_i = green[0].astype(F32), green[1].astype(F32)
+        trace_w[...] = 0.5 * ((f_i - f_r) + (f_i + f_r).T)
+
+    def own_maps():
+        prepare(0, maps[core, 0], maps[core, 1])
+
+        @pl.when(core == 1)
+        def _():
+            prepare(1, maps[0, 0], maps[0, 1])
+
+        trace_weights()
 
     def multiply(slot, ref):
         real, imag = split(ref[0]), split(ref[1])
@@ -262,11 +280,11 @@
     def _():
         prepare(2, pair_map[0], pair_map[1])
 
-    prepare(0, maps[core, 0], maps[core, 1])
-
-    @pl.when(core == 1)
+    opens = jnp.logical_and(tail == 0, place == 0)
+
+    @pl.when(jnp.logical_not(opens))
     def _():
-        prepare(1, maps[0, 0], maps[0, 1])
+        own_maps()
 
     def flow():
         weight_u = 0.5 * (coupling[0].astype(F32) - coupling[1].astype(F32))
@@ -333,6 +351,7 @@
                     at = chunk_rows(chunk)
                     head_out[at, :] = second(2, chunk) + pair_source[at, :]
                 head_source_copy.start()
+                own_maps()
                 for chunk in range(CHUNKS):
                     load(chain_in, chunk)
 
@@ -387,7 +406,9 @@
             for chunk in range(CHUNKS):
                 load(state_in, chunk)
 
-        first(0)
+        @pl.when(jnp.logical_or(core == 0, jnp.logical_not(ends)))
+        def _():
+            first(0)
 
         @pl.when(jnp.logical_not(ends))
         def _():

time: 44.6 us -> 43.5 us (0.975)
  Pallas kernels: 38.3 us -> 37.2 us
    pallas_call x1, Pallas kernels: 38.3 us -> 37.2 us  [on_device(): pl.pallas_call(kernel, out_shape=(jax.ShapeDtypeStruct((2, n, n), F32), j...]
where the time goes in v4:
time: 43.5 us; the launch traced here: 43.3 us
  Pallas kernels  37.2 us (86%)
  between operations  4.27 us (10%)
  local copies, waits for them, and re-layouts  1.87 us (4%)
    pallas_call x1, Pallas kernels, on_device(): pl.pallas_call(kernel, out_shape=(jax.ShapeDtypeStruct((2, n, n), F32), j...  37.2 us
    unnamed x1, local copies, waits for them, and re-layouts  1.87 us

profile of v4, /device:TPU:1, one launch (start us, length us, event | category | flops | bytes accessed | tf_op | source)
XLA Modules:
  0.0 43.3 jit_solution(1078458372511763017)
XLA Ops:
  2.6 37.2 %shard_map.77 = (f32[2,256,256]{2,1,0:T(8,128)}, f32[1]{0:T(128)}) custom-call(bf16[2,256,256]{2,1,0:T(8,128)(2,1)} %bitcast.4, bf16[2,256,256]{2,1,0:T(8,128)(2,1)} %bitcast.5, f32[1,256]{1,0:T(1,128)} %gamma_in.1, f32[1,1]{1,0:T(1,128)S(6)} %copy.10.occupation, f32[1]{0:T(128)S(6)} %copy.11.lead_occ, f32[1]{0:T(128)S(6)} %copy.12.energy_weight), custom_call_target="tpu_custom_call" | custom-call | tf_op jit(solution)/shard_map/pallas_call | solution.py:489
  39.8 1.9 %copy.13 = f32[1,1,2,256,256]{4,3,2,1,0:T(8,128)} copy(f32[1,1,2,256,256]{4,3,2,1,0:T(8,128)} %bitcast.3) | data formatting | bytes 1048576

commit v5 on v4

--- a/solution.py
+++ b/solution.py
@@ -301,24 +301,27 @@
         out[1] = 0.5 * (block - turned)
 
     def relay(slot, source):
+        near_first = jnp.logical_and(place == last - 1, core == 0)
+        far_first = jnp.logical_and(place < last, jnp.logical_not(near_first))
+
         for chunk in range(CHUNKS):
             at = chunk_rows(chunk)
             chain_out[at, :] = second(slot, chunk) + source[at, :]
 
-            @pl.when(place < last - 1)
+            @pl.when(far_first)
             def _():
                 chain_copy(chunk, 0).start()
 
-            @pl.when(place == last - 1)
+            @pl.when(near_first)
             def _():
                 chain_copy(chunk, 1).start()
 
         for chunk in range(CHUNKS):
-            @pl.when(place < last - 1)
+            @pl.when(far_first)
             def _():
                 chain_copy(chunk, 1).start()
 
-            @pl.when(place == last - 1)
+            @pl.when(near_first)
             def _():
                 chain_copy(chunk, 0).start()
 

time: 43.5 us -> 42.4 us (0.975)
  the two profiles are of different devices: /device:TPU:1 before, /device:TPU:31 now
where the time goes in v5:
time: 42.4 us; the launch traced here: 42.2 us
  Pallas kernels  36 us (85%)
  between operations  4.27 us (10%)
  local copies, waits for them, and re-layouts  1.87 us (4%)
    pallas_call x1, Pallas kernels, on_device(): pl.pallas_call(kernel, out_shape=(jax.ShapeDtypeStruct((2, n, n), F32), j...  36 us
    unnamed x1, local copies, waits for them, and re-layouts  1.87 us

profile of v5, /device:TPU:31, one launch (start us, length us, event | category | flops | bytes accessed | tf_op | source)
XLA Modules:
  0.0 42.2 jit_solution(11212963505497805476)
XLA Ops:
  2.6 36.0 %shard_map.77 = (f32[2,256,256]{2,1,0:T(8,128)}, f32[1]{0:T(128)}) custom-call(bf16[2,256,256]{2,1,0:T(8,128)(2,1)} %bitcast.4, bf16[2,256,256]{2,1,0:T(8,128)(2,1)} %bitcast.5, f32[1,256]{1,0:T(1,128)} %gamma_in.1, f32[1,1]{1,0:T(1,128)S(6)} %copy.10.occupation, f32[1]{0:T(128)S(6)} %copy.11.lead_occ, f32[1]{0:T(128)S(6)} %copy.12.energy_weight), custom_call_target="tpu_custom_call" | custom-call | tf_op jit(solution)/shard_map/pallas_call | solution.py:492
  38.6 1.9 %copy.13 = f32[1,1,2,256,256]{4,3,2,1,0:T(8,128)} copy(f32[1,1,2,256,256]{4,3,2,1,0:T(8,128)} %bitcast.3) | data formatting | bytes 1048576
